TPU v7x, 512 devices: a whole 4x4x16 slice. The times are simulated.
512 devices in a mesh: seq: 128 (over z, x, core), head: 4 (over y).
Axes of the slice: x: 4, y: 4, z: 16, core: 2. Of those that a mesh axis runs over, the one named last changes fastest.
Arguments:
- queries: bfloat16 [32768, 4096], P('seq', 'head'), may hold values from -100 to 100
- keys_values: bfloat16 [32768, 2, 512], P('seq', None, 'head'), may hold values from -4.5 to 4.5
- cache_kv: bfloat16 [32768, 2, 512], P('seq', None, 'head'), may hold values from -4 to 4
- vertical_pages: int32 [4, 4], P('head'), may hold values from 0 to 255, as said below
- slash_shift: int32 [4, 3], P('head'), may hold values from 1 to 128, as said below
- slash_live: int32 [128, 4, 3], P('seq', 'head'), may hold values 0 or 1
- out_proj: bfloat16 [4096, 2048], P('head'), may hold values from -0.09375 to 0.09375
Outputs:
- projected: bfloat16 [32768, 2048], P('seq', 'head')
Inputs may be any that keep to these rules, and one draw needn't show every extreme that they name: `vertical_pages`: each head group lists 4 distinct pages. `slash_shift`: each head group lists 3 distinct distances.
All inputs are finite; a program needn't handle non-finite values. No bound on the sum of `slash_live` on one device may be relied on, other than what follows from the above.
Results may differ from a plain program's by a relative error of at most 0.0057.
Values may be sent and summed in bfloat16 or wider, within the bound.
A program may use at most 64 MiB of HBM per device.

v0:
```python
import jax
import jax.numpy as jnp
from jax import lax
from jax.sharding import PartitionSpec as P

PAGE = 128


def passed_along(value, axis, steps):
    count = lax.axis_size(axis)
    pairs = [(source, (source + steps) % count) for source in range(count)]
    return lax.ppermute(value, axis, pairs)


def broadcast(value, axis, source):
    kept = jnp.where(lax.axis_index(axis) == source, value, 0).astype(value.dtype)
    return lax.psum(kept, axis)


def rotate(stacked, amounts, shards):
    reduced = amounts % shards
    for bit_number in range(max(1, (shards - 1).bit_length())):
        moved = passed_along(stacked, "seq", 1 << bit_number)
        chosen = reduced // (1 << bit_number) % 2 == 1
        stacked = jnp.where(chosen[:, None, None, None], moved, stacked)
    return stacked


def body(queries, keys_values, cache_kv, vertical_pages, slash_shift, slash_live, out_proj):
    row_count = queries.shape[0]
    head_width = keys_values.shape[2]
    group_heads = queries.shape[1] // head_width
    shards = lax.axis_size("seq")
    own_shard = lax.axis_index("seq")
    distances = slash_shift[0]
    live_blocks = slash_live[0, 0] == 1
    page_ids = vertical_pages[0]
    slash_count = distances.shape[0]
    payload = jnp.where(
        (own_shard < shards - distances)[:, None, None, None], keys_values[None], cache_kv[None]
    )
    slash_kv = jnp.concatenate(
        [
            rotate(payload[position : position + 1], distances[position : position + 1], shards)
            for position in range(slash_count)
        ],
        0,
    )
    per_shard = row_count // PAGE
    owners = page_ids // per_shard
    offsets = page_ids % per_shard * PAGE
    copies = []
    for position in range(page_ids.shape[0]):
        own_page = lax.dynamic_slice_in_dim(cache_kv, offsets[position], PAGE, 0)
        copies.append(broadcast(own_page, "seq", owners[position]))
    vertical = jnp.stack(copies, 0)
    cached_slash = own_shard + shards - distances
    clash = (
        live_blocks[None, :]
        & (distances[None, :] > own_shard)
        & (owners[:, None] == cached_slash[None, :])
    )
    page_open = jnp.logical_not(jnp.any(clash, axis=1))
    row_ids = lax.broadcasted_iota(jnp.int32, (row_count, row_count), 0)
    col_ids = lax.broadcasted_iota(jnp.int32, (row_count, row_count), 1)
    causal = row_ids >= col_ids
    column_open = jnp.concatenate([jnp.repeat(live_blocks, row_count), jnp.repeat(page_open, PAGE)])
    visible = jnp.concatenate(
        [causal, jnp.broadcast_to(column_open[None, :], (row_count, column_open.shape[0]))], 1
    )
    all_keys = jnp.concatenate(
        [keys_values, slash_kv.reshape(-1, 2, head_width), vertical.reshape(-1, 2, head_width)], 0
    )
    query_heads = queries.reshape(row_count, group_heads, head_width)
    scores = jnp.einsum(
        "rgd,kd->grk", query_heads, all_keys[:, 0, :], preferred_element_type=jnp.float32
    )
    scores = scores * head_width ** (-0.5)
    scores = jnp.where(visible[None], scores, -jnp.inf)
    row_max = jnp.max(scores, axis=2, keepdims=True)
    weights = jnp.exp(scores - row_max)
    row_total = jnp.sum(weights, axis=2, keepdims=True)
    weights_bf = (weights / row_total).astype(jnp.bfloat16)
    attended = jnp.einsum(
        "grk,kd->rgd", weights_bf, all_keys[:, 1, :], preferred_element_type=jnp.float32
    )
    attended = attended.astype(jnp.bfloat16).reshape(row_count, group_heads * head_width)
    group_terms = jnp.dot(attended, out_proj, preferred_element_type=jnp.float32)
    return lax.psum_scatter(group_terms, "head", scatter_dimension=1, tiled=True).astype(
        jnp.bfloat16
    )


def solution(mesh):
    placed = (
        P("seq", "head"),
        P("seq", None, "head"),
        P("seq", None, "head"),
        P("head", None),
        P("head", None),
        P("seq", "head", None),
        P("head", None),
    )
    return jax.shard_map(
        body, mesh=mesh, in_specs=placed, out_specs=P("seq", "head"), check_vma=False
    )
```

profile of v0, /device:TPU:1, one launch (start us, length us, event | category | flops | bytes accessed | tf_op | source)
XLA Modules:
  0.0 558.2 jit_solution(9154548821410170501)
XLA Ops:
  6.5 1.0 copy.18
  7.5 0.9 copy.16
  8.5 0.7 compare_bitcast_fusion
  9.1 0.1 broadcast_select_fusion
  9.3 4.5 collective-permute-start
  13.8 1.9 collective-permute-start.14
  15.7 3.5 collective-permute-start.7
  19.2 0.7 fusion.25
  19.9 0.7 fusion.30
  30.8 1.8 fusion.20
  32.6 0.0 reduce-scatter.2.cloned.1.call-start
  32.7 0.7 compare_bitcast_fusion.1
  33.4 0.7 subtract_bitcast_fusion
  34.1 0.1 broadcast_in_dim.281
  34.1 0.2 and_reduce_fusion
  34.3 0.1 broadcast_bitcast_fusion
  34.4 0.3 pad_add_fusion
  34.7 1.4 fusion.29
  42.1 2.8 collective-permute-start.1
  45.3 319.2 %all-reduce.3.cloned.1.call-done = (bf16[1,128,2,128]{3,2,1,0:T(2,128)(2,1)}, bf16[1,128,2,128]{3,2,1,0:T(2,128)(2,1)}, bf16[1,128,2,128]{3,2,1,0:T(2,128)(2,1)}, bf16[1,128,2,128]{3,2,1,0:T(2,128)(2,1)}) async-done(((bf16[1,128,2,128]{3,2,1,0:T(2,128)(2,1)}, bf16[1,128,2,128]{3,2,1,0:T(2,128)(2,1)}, bf16[1,128,2,128]{3,2,1,0:T(2,128)(2,1)}, bf16[1,128,2,128]{3,2,1,0:T(2,128)(2,1)}), ...) | async-done | bytes 262160 | tf_op jit(solution)/shard_map/psum | solution.py:17
  364.5 1.4 pad_maximum_fusion.2
  365.9 2.8 collective-permute-start.8
  368.7 2.4 collective-permute-start.15
  371.2 4.5 collective-permute-start.2
  375.7 2.0 collective-permute-start.9
  377.6 0.8 collective-permute-done.15
  378.5 4.4 collective-permute-start.16
  382.9 4.2 collective-permute-start.3
  387.2 1.9 collective-permute-start.10
  389.2 2.7 collective-permute-start.17
  391.9 5.5 collective-permute-start.4
  397.4 2.6 collective-permute-start.11
  400.0 3.9 collective-permute-start.18
  404.0 3.9 collective-permute-start.5
  407.9 6.1 %collective-permute-start.12 = (bf16[1,256,2,128]{3,1,0,2:T(8,128)(2,1)S(1)}, bf16[1,256,2,128]{3,1,0,2:T(8,128)(2,1)S(1)}, u32[]{:S(2)}, u32[]{:S(2)}) collective-permute-start(bf16[1,256,2,128]{3,1,0,2:T(8,128)(2,1)S(1)} %broadcast_select_fusion.16), channel_id=1, source_target_pairs={{0,128},{4,132},{8,136},{12,140},{16,144},{20,148},{24,152},{28,15... | collective-permute-start | bytes 393224 | tf_op jit(solution)/shard_map/ppermute | solution.py:12
  414.0 4.2 collective-permute-start.19
  418.3 8.7 %collective-permute-start.6 = (bf16[1,256,2,128]{3,1,0,2:T(8,128)(2,1)S(1)}, bf16[1,256,2,128]{3,1,0,2:T(8,128)(2,1)S(1)}, u32[]{:S(2)}, u32[]{:S(2)}) collective-permute-start(bf16[1,256,2,128]{3,1,0,2:T(8,128)(2,1)S(1)} %broadcast_select_fusion.24), channel_id=1, source_target_pairs={{0,256},{4,260},{8,264},{12,268},{16,272},{20,276},{24,280},{28,28... | collective-permute-start | bytes 393224 | tf_op jit(solution)/shard_map/ppermute | solution.py:12
  427.0 5.3 collective-permute-start.13
  432.4 8.7 %collective-permute-start.20 = (bf16[1,256,2,128]{3,1,0,2:T(8,128)(2,1)S(1)}, bf16[1,256,2,128]{3,1,0,2:T(8,128)(2,1)S(1)}, u32[]{:S(2)}, u32[]{:S(2)}) collective-permute-start(bf16[1,256,2,128]{3,1,0,2:T(8,128)(2,1)S(1)} %broadcast_select_fusion.10), channel_id=1, source_target_pairs={{0,256},{4,260},{8,264},{12,268},{16,272},{20,276},{24,280},{28,28... | collective-permute-start | bytes 393224 | tf_op jit(solution)/shard_map/ppermute | solution.py:12
  441.1 10.1 %collective-permute-done.13 = bf16[1,256,2,128]{3,1,0,2:T(8,128)(2,1)S(1)} collective-permute-done((bf16[1,256,2,128]{3,1,0,2:T(8,128)(2,1)S(1)}, bf16[1,256,2,128]{3,1,0,2:T(8,128)(2,1)S(1)}, u32[]{:S(2)}, u32[]{:S(2)}) %collective-permute-start.13) | collective-permute-done | bytes 131104 | tf_op jit(solution)/shard_map/ppermute | solution.py:12
  451.2 10.7 %collective-permute-done.20 = bf16[1,256,2,128]{3,1,0,2:T(8,128)(2,1)S(1)} collective-permute-done((bf16[1,256,2,128]{3,1,0,2:T(8,128)(2,1)S(1)}, bf16[1,256,2,128]{3,1,0,2:T(8,128)(2,1)S(1)}, u32[]{:S(2)}, u32[]{:S(2)}) %collective-permute-start.20) | collective-permute-done | bytes 131104 | tf_op jit(solution)/shard_map/ppermute | solution.py:12
  461.9 0.1 pad_maximum_fusion
  462.0 6.9 %fusion.32 = (f32[8,256]{1,0:T(8,128)S(1)}, f32[8,256,1536]{1,2,0:T(8,128)}) fusion(pred[256,1536]{0,1:T(8,128)(4,1)S(1)} %pad_add_fusion, bf16[1536,2,128]{2,0,1:T(8,128)(2,1)S(1)} %pad_maximum_fusion, bf16[256,1024]{1,0:T(8,128)(2,1)S(1)} %copy-done), kind=kOutput, calls=%fused_computation.74 | convolution fusion | flops 817890816 | bytes 13901824 | tf_op jit(solution)/shard_map/sub | solution.py:81
  468.9 5.7 %fusion.8 = bf16[128,8,256]{2,0,1:T(8,128)(2,1)S(1)} fusion(f32[8,256,1536]{1,2,0:T(8,128)} %get-tuple-element.35, f32[8,256]{1,0:T(8,128)S(1)} %get-tuple-element.34, bf16[1536,2,128]{2,0,1:T(8,128)(2,1)S(1)} %pad_maximum_fusion), kind=kOutput, calls=%fused_computation.11 | convolution fusion | flops 811859968 | bytes 13508608 | tf_op jit(solution)/shard_map/grk,kd->rgd/dot_general | solution.py:84
  474.6 0.0 copy-done.1
  474.7 2.6 fusion.37
  477.3 72.3 %reduce-scatter.2.cloned.1.call-done = f32[256,512]{1,0:T(8,128)} async-done(((f32[256,2048]{1,0:T(8,128)}), f32[256,512]{1,0:T(8,128)}) %reduce-scatter.2.cloned.1.call-update) | async-done | bytes 524304 | tf_op jit(solution)/shard_map/reduce_scatter | solution.py:89
  549.6 1.8 convert_element_type.20
  (51 shorter events, 0.6 us)
Async XLA Ops:
  6.5 455.4 %copy-start = (bf16[256,1024]{1,0:T(8,128)(2,1)S(1)}, bf16[256,1024]{1,0:T(8,128)(2,1)}, u32[]{:S(2)}) copy-start(bf16[256,1024]{1,0:T(8,128)(2,1)} %param.7) | copy-start | bytes 1572868
  6.5 357.9 %all-reduce.3.cloned.1.call-start = ((), (), s32[]{:S(2)}) async-start(), calls=%async_computation.2 | async-start | bytes 524288 | tf_op jit(solution)/shard_map/psum | solution.py:17
  9.3 32.7 %collective-permute-start = (bf16[1,256,2,128]{3,1,0,2:T(8,128)(2,1)S(1)}, bf16[1,256,2,128]{3,1,0,2:T(8,128)(2,1)S(1)}, u32[]{:S(2)}, u32[]{:S(2)}) collective-permute-start(bf16[1,256,2,128]{3,1,0,2:T(8,128)(2,1)S(1)} %get-tuple-element.12), channel_id=1, source_target_pairs={{0,4},{4,8},{8,12},{12,16},{16,20},{20,24},{24,28},{28,32},{32,36}... | collective-permute-start | bytes 393224 | tf_op jit(solution)/shard_map/ppermute | solution.py:12
  13.8 28.2 %collective-permute-start.14 = (bf16[1,256,2,128]{3,1,0,2:T(8,128)(2,1)S(1)}, bf16[1,256,2,128]{3,1,0,2:T(8,128)(2,1)S(1)}, u32[]{:S(2)}, u32[]{:S(2)}) collective-permute-start(bf16[1,256,2,128]{3,1,0,2:T(8,128)(2,1)S(1)} %get-tuple-element.13), channel_id=1, source_target_pairs={{0,4},{4,8},{8,12},{12,16},{16,20},{20,24},{24,28},{28,32},{32,36}... | collective-permute-start | bytes 393224 | tf_op jit(solution)/shard_map/ppermute | solution.py:12
  15.7 26.3 %collective-permute-start.7 = (bf16[1,256,2,128]{3,1,0,2:T(8,128)(2,1)S(1)}, bf16[1,256,2,128]{3,1,0,2:T(8,128)(2,1)S(1)}, u32[]{:S(2)}, u32[]{:S(2)}) collective-permute-start(bf16[1,256,2,128]{3,1,0,2:T(8,128)(2,1)S(1)} %get-tuple-element.14), channel_id=1, source_target_pairs={{0,4},{4,8},{8,12},{12,16},{16,20},{20,24},{24,28},{28,32},{32,36}... | collective-permute-start | bytes 393224 | tf_op jit(solution)/shard_map/ppermute | solution.py:12
  32.6 517.0 %reduce-scatter.2.cloned.1.call-start = ((), (), s32[]{:S(2)}) async-start(), calls=%async_computation.1 | async-start | bytes 2621440 | tf_op jit(solution)/shard_map/reduce_scatter | solution.py:89
  42.1 329.1 %collective-permute-start.1 = (bf16[1,256,2,128]{3,1,0,2:T(8,128)(2,1)S(1)}, bf16[1,256,2,128]{3,1,0,2:T(8,128)(2,1)S(1)}, u32[]{:S(2)}, u32[]{:S(2)}) collective-permute-start(bf16[1,256,2,128]{3,1,0,2:T(8,128)(2,1)S(1)} %get-tuple-element.9), channel_id=1, source_target_pairs={{0,8},{4,12},{8,16},{12,20},{16,24},{20,28},{24,32},{28,36},{32,40... | collective-permute-start | bytes 393224 | tf_op jit(solution)/shard_map/ppermute | solution.py:12
  365.9 9.7 %collective-permute-start.8 = (bf16[1,256,2,128]{3,1,0,2:T(8,128)(2,1)S(1)}, bf16[1,256,2,128]{3,1,0,2:T(8,128)(2,1)S(1)}, u32[]{:S(2)}, u32[]{:S(2)}) collective-permute-start(bf16[1,256,2,128]{3,1,0,2:T(8,128)(2,1)S(1)} %get-tuple-element.10), channel_id=1, source_target_pairs={{0,8},{4,12},{8,16},{12,20},{16,24},{20,28},{24,32},{28,36},{32,40... | collective-permute-start | bytes 393224 | tf_op jit(solution)/shard_map/ppermute | solution.py:12
  368.7 9.7 %collective-permute-start.15 = (bf16[1,256,2,128]{3,1,0,2:T(8,128)(2,1)S(1)}, bf16[1,256,2,128]{3,1,0,2:T(8,128)(2,1)S(1)}, u32[]{:S(2)}, u32[]{:S(2)}) collective-permute-start(bf16[1,256,2,128]{3,1,0,2:T(8,128)(2,1)S(1)} %get-tuple-element.11), channel_id=1, source_target_pairs={{0,8},{4,12},{8,16},{12,20},{16,24},{20,28},{24,32},{28,36},{32,40... | collective-permute-start | bytes 393224 | tf_op jit(solution)/shard_map/ppermute | solution.py:12
  371.2 11.7 %collective-permute-start.2 = (bf16[1,256,2,128]{3,1,0,2:T(8,128)(2,1)S(1)}, bf16[1,256,2,128]{3,1,0,2:T(8,128)(2,1)S(1)}, u32[]{:S(2)}, u32[]{:S(2)}) collective-permute-start(bf16[1,256,2,128]{3,1,0,2:T(8,128)(2,1)S(1)} %broadcast_select_fusion.20), channel_id=1, source_target_pairs={{0,16},{4,20},{8,24},{12,28},{16,32},{20,36},{24,40},{28,44},{32,4... | collective-permute-start | bytes 393224 | tf_op jit(solution)/shard_map/ppermute | solution.py:12
  375.7 11.5 %collective-permute-start.9 = (bf16[1,256,2,128]{3,1,0,2:T(8,128)(2,1)S(1)}, bf16[1,256,2,128]{3,1,0,2:T(8,128)(2,1)S(1)}, u32[]{:S(2)}, u32[]{:S(2)}) collective-permute-start(bf16[1,256,2,128]{3,1,0,2:T(8,128)(2,1)S(1)} %broadcast_select_fusion.13), channel_id=1, source_target_pairs={{0,16},{4,20},{8,24},{12,28},{16,32},{20,36},{24,40},{28,44},{32,4... | collective-permute-start | bytes 393224 | tf_op jit(solution)/shard_map/ppermute | solution.py:12
  378.5 10.6 %collective-permute-start.16 = (bf16[1,256,2,128]{3,1,0,2:T(8,128)(2,1)S(1)}, bf16[1,256,2,128]{3,1,0,2:T(8,128)(2,1)S(1)}, u32[]{:S(2)}, u32[]{:S(2)}) collective-permute-start(bf16[1,256,2,128]{3,1,0,2:T(8,128)(2,1)S(1)} %broadcast_select_fusion.6), channel_id=1, source_target_pairs={{0,16},{4,20},{8,24},{12,28},{16,32},{20,36},{24,40},{28,44},{32,4... | collective-permute-start | bytes 393224 | tf_op jit(solution)/shard_map/ppermute | solution.py:12
  382.9 8.9 %collective-permute-start.3 = (bf16[1,256,2,128]{3,1,0,2:T(8,128)(2,1)S(1)}, bf16[1,256,2,128]{3,1,0,2:T(8,128)(2,1)S(1)}, u32[]{:S(2)}, u32[]{:S(2)}) collective-permute-start(bf16[1,256,2,128]{3,1,0,2:T(8,128)(2,1)S(1)} %broadcast_select_fusion.21), channel_id=1, source_target_pairs={{0,32},{4,36},{8,40},{12,44},{16,48},{20,52},{24,56},{28,60},{32,6... | collective-permute-start | bytes 393224 | tf_op jit(solution)/shard_map/ppermute | solution.py:12
  387.2 10.2 %collective-permute-start.10 = (bf16[1,256,2,128]{3,1,0,2:T(8,128)(2,1)S(1)}, bf16[1,256,2,128]{3,1,0,2:T(8,128)(2,1)S(1)}, u32[]{:S(2)}, u32[]{:S(2)}) collective-permute-start(bf16[1,256,2,128]{3,1,0,2:T(8,128)(2,1)S(1)} %broadcast_select_fusion.14), channel_id=1, source_target_pairs={{0,32},{4,36},{8,40},{12,44},{16,48},{20,52},{24,56},{28,60},{32,6... | collective-permute-start | bytes 393224 | tf_op jit(solution)/shard_map/ppermute | solution.py:12
  389.2 10.8 %collective-permute-start.17 = (bf16[1,256,2,128]{3,1,0,2:T(8,128)(2,1)S(1)}, bf16[1,256,2,128]{3,1,0,2:T(8,128)(2,1)S(1)}, u32[]{:S(2)}, u32[]{:S(2)}) collective-permute-start(bf16[1,256,2,128]{3,1,0,2:T(8,128)(2,1)S(1)} %broadcast_select_fusion.7), channel_id=1, source_target_pairs={{0,32},{4,36},{8,40},{12,44},{16,48},{20,52},{24,56},{28,60},{32,6... | collective-permute-start | bytes 393224 | tf_op jit(solution)/shard_map/ppermute | solution.py:12
  391.9 12.1 %collective-permute-start.4 = (bf16[1,256,2,128]{3,1,0,2:T(8,128)(2,1)S(1)}, bf16[1,256,2,128]{3,1,0,2:T(8,128)(2,1)S(1)}, u32[]{:S(2)}, u32[]{:S(2)}) collective-permute-start(bf16[1,256,2,128]{3,1,0,2:T(8,128)(2,1)S(1)} %broadcast_select_fusion.22), channel_id=1, source_target_pairs={{0,64},{4,68},{8,72},{12,76},{16,80},{20,84},{24,88},{28,92},{32,9... | collective-permute-start | bytes 393224 | tf_op jit(solution)/shard_map/ppermute | solution.py:12
  397.4 10.5 %collective-permute-start.11 = (bf16[1,256,2,128]{3,1,0,2:T(8,128)(2,1)S(1)}, bf16[1,256,2,128]{3,1,0,2:T(8,128)(2,1)S(1)}, u32[]{:S(2)}, u32[]{:S(2)}) collective-permute-start(bf16[1,256,2,128]{3,1,0,2:T(8,128)(2,1)S(1)} %broadcast_select_fusion.15), channel_id=1, source_target_pairs={{0,64},{4,68},{8,72},{12,76},{16,80},{20,84},{24,88},{28,92},{32,9... | collective-permute-start | bytes 393224 | tf_op jit(solution)/shard_map/ppermute | solution.py:12
  400.0 14.0 %collective-permute-start.18 = (bf16[1,256,2,128]{3,1,0,2:T(8,128)(2,1)S(1)}, bf16[1,256,2,128]{3,1,0,2:T(8,128)(2,1)S(1)}, u32[]{:S(2)}, u32[]{:S(2)}) collective-permute-start(bf16[1,256,2,128]{3,1,0,2:T(8,128)(2,1)S(1)} %broadcast_select_fusion.8), channel_id=1, source_target_pairs={{0,64},{4,68},{8,72},{12,76},{16,80},{20,84},{24,88},{28,92},{32,9... | collective-permute-start | bytes 393224 | tf_op jit(solution)/shard_map/ppermute | solution.py:12
  404.0 14.2 %collective-permute-start.5 = (bf16[1,256,2,128]{3,1,0,2:T(8,128)(2,1)S(1)}, bf16[1,256,2,128]{3,1,0,2:T(8,128)(2,1)S(1)}, u32[]{:S(2)}, u32[]{:S(2)}) collective-permute-start(bf16[1,256,2,128]{3,1,0,2:T(8,128)(2,1)S(1)} %broadcast_select_fusion.23), channel_id=1, source_target_pairs={{0,128},{4,132},{8,136},{12,140},{16,144},{20,148},{24,152},{28,15... | collective-permute-start | bytes 393224 | tf_op jit(solution)/shard_map/ppermute | solution.py:12
  407.9 19.1 %collective-permute-start.12 = (bf16[1,256,2,128]{3,1,0,2:T(8,128)(2,1)S(1)}, bf16[1,256,2,128]{3,1,0,2:T(8,128)(2,1)S(1)}, u32[]{:S(2)}, u32[]{:S(2)}) collective-permute-start(bf16[1,256,2,128]{3,1,0,2:T(8,128)(2,1)S(1)} %broadcast_select_fusion.16), channel_id=1, source_target_pairs={{0,128},{4,132},{8,136},{12,140},{16,144},{20,148},{24,152},{28,15... | collective-permute-start | bytes 393224 | tf_op jit(solution)/shard_map/ppermute | solution.py:12
  414.0 18.3 %collective-permute-start.19 = (bf16[1,256,2,128]{3,1,0,2:T(8,128)(2,1)S(1)}, bf16[1,256,2,128]{3,1,0,2:T(8,128)(2,1)S(1)}, u32[]{:S(2)}, u32[]{:S(2)}) collective-permute-start(bf16[1,256,2,128]{3,1,0,2:T(8,128)(2,1)S(1)} %broadcast_select_fusion.9), channel_id=1, source_target_pairs={{0,128},{4,132},{8,136},{12,140},{16,144},{20,148},{24,152},{28,15... | collective-permute-start | bytes 393224 | tf_op jit(solution)/shard_map/ppermute | solution.py:12
  418.3 22.8 %collective-permute-start.6 = (bf16[1,256,2,128]{3,1,0,2:T(8,128)(2,1)S(1)}, bf16[1,256,2,128]{3,1,0,2:T(8,128)(2,1)S(1)}, u32[]{:S(2)}, u32[]{:S(2)}) collective-permute-start(bf16[1,256,2,128]{3,1,0,2:T(8,128)(2,1)S(1)} %broadcast_select_fusion.24), channel_id=1, source_target_pairs={{0,256},{4,260},{8,264},{12,268},{16,272},{20,276},{24,280},{28,28... | collective-permute-start | bytes 393224 | tf_op jit(solution)/shard_map/ppermute | solution.py:12
  427.0 24.1 %collective-permute-start.13 = (bf16[1,256,2,128]{3,1,0,2:T(8,128)(2,1)S(1)}, bf16[1,256,2,128]{3,1,0,2:T(8,128)(2,1)S(1)}, u32[]{:S(2)}, u32[]{:S(2)}) collective-permute-start(bf16[1,256,2,128]{3,1,0,2:T(8,128)(2,1)S(1)} %broadcast_select_fusion.17), channel_id=1, source_target_pairs={{0,256},{4,260},{8,264},{12,268},{16,272},{20,276},{24,280},{28,28... | collective-permute-start | bytes 393224 | tf_op jit(solution)/shard_map/ppermute | solution.py:12
  432.4 29.5 %collective-permute-start.20 = (bf16[1,256,2,128]{3,1,0,2:T(8,128)(2,1)S(1)}, bf16[1,256,2,128]{3,1,0,2:T(8,128)(2,1)S(1)}, u32[]{:S(2)}, u32[]{:S(2)}) collective-permute-start(bf16[1,256,2,128]{3,1,0,2:T(8,128)(2,1)S(1)} %broadcast_select_fusion.10), channel_id=1, source_target_pairs={{0,256},{4,260},{8,264},{12,268},{16,272},{20,276},{24,280},{28,28... | collective-permute-start | bytes 393224 | tf_op jit(solution)/shard_map/ppermute | solution.py:12
  468.9 5.8 %copy-start.1 = (bf16[1024,2048]{1,0:T(8,128)(2,1)S(1)}, bf16[1024,2048]{1,0:T(8,128)(2,1)}, u32[]{:S(2)}) copy-start(bf16[1024,2048]{1,0:T(8,128)(2,1)} %param.13) | copy-start | bytes 12582916
Sparse Core Ops, SparseCore 0:
  32.8 331.6 all-reduce.2
  477.4 72.1 reduce-scatter.1
where the time goes:
time: 559 us; the launch traced here: 558 us
  waiting for transfers between devices  413 us (74%)
  starting transfers between devices  86.4 us (15%)
  between operations  30.4 us (5%)
  matrix products  15.3 us (3%)
  other arithmetic  8.74 us (2%)
    psum x1, waiting for transfers between devices, broadcast(): return lax.psum(kept, axis)  319 us
    ppermute x21, starting transfers between devices, passed_along(): return lax.ppermute(value, axis, pairs)  86.4 us
    reduce_scatter x1, waiting for transfers between devices, body(): lax.psum_scatter(group_terms, 'head', scatter_dimension=1, tiled=True)  72.3 us
    ppermute x21, waiting for transfers between devices, passed_along(): return lax.ppermute(value, axis, pairs)  21.6 us
  transfers between devices with their start and end apart: 23, of which 5 were waited for; matrix products, arithmetic and copies ran while one was open for 2% of the time, Pallas kernels for 0%

commit v1 on v0

--- a/solution.py
+++ b/solution.py
@@ -14,7 +14,7 @@
 
 def broadcast(value, axis, source):
     kept = jnp.where(lax.axis_index(axis) == source, value, 0).astype(value.dtype)
-    return lax.psum(kept, axis)
+    return jnp.sum(lax.all_gather(kept, axis), axis=0)
 
 
 def rotate(stacked, amounts, shards):

time: 559 us -> 710 us (1.27)
  waiting for transfers between devices: 413 us -> 519 us
  other arithmetic: 8.74 us -> 42.9 us
  starting transfers between devices: 86.4 us -> 97.1 us
    all_gather x0 -> x4, waiting for transfers between devices: none -> 453 us  [broadcast(): return jnp.sum(lax.all_gather(kept, axis), axis=0)]
    psum x1 -> x0, waiting for transfers between devices: 319 us -> none  [broadcast(): return lax.psum(kept, axis)]
    reduce_scatter x1, waiting for transfers between devices: 72.3 us -> 32.2 us  [body(): lax.psum_scatter(group_terms, 'head', scatter_dimension=1, tiled=True)]
    reduce_sum x0 -> x4, other arithmetic: none -> 35 us  [broadcast(): return jnp.sum(lax.all_gather(kept, axis), axis=0)]
    ppermute x21, starting transfers between devices: 86.4 us -> 97 us  [passed_along(): return lax.ppermute(value, axis, pairs)]
    ppermute x21, waiting for transfers between devices: 21.6 us -> 31.6 us  [passed_along(): return lax.ppermute(value, axis, pairs)]
  transfers between devices with their start and end apart: 23 -> 26, of which waited for: 5 -> 11; matrix products, arithmetic and copies ran while one was open for 2% -> 5% of each run, Pallas kernels for 0% -> 0%
where the time goes in v1:
time: 710 us; the launch traced here: 709 us
  waiting for transfers between devices  519 us (73%)
  starting transfers between devices  97.1 us (14%)
  other arithmetic  42.9 us (6%)
  between operations  30.2 us (4%)
  matrix products  15.2 us (2%)
    all_gather x4, waiting for transfers between devices, broadcast(): return jnp.sum(lax.all_gather(kept, axis), axis=0)  453 us
    ppermute x21, starting transfers between devices, passed_along(): return lax.ppermute(value, axis, pairs)  97 us
    reduce_sum x4, other arithmetic, broadcast(): return jnp.sum(lax.all_gather(kept, axis), axis=0)  35 us
    reduce_scatter x1, waiting for transfers between devices, body(): lax.psum_scatter(group_terms, 'head', scatter_dimension=1, tiled=True)  32.2 us
    ppermute x21, waiting for transfers between devices, passed_along(): return lax.ppermute(value, axis, pairs)  31.6 us
  transfers between devices with their start and end apart: 26, of which 11 were waited for; matrix products, arithmetic and copies ran while one was open for 5% of the time, Pallas kernels for 0%

profile of v1, /device:TPU:1, one launch (start us, length us, event | category | flops | bytes accessed | tf_op | source)
XLA Modules:
  0.0 708.7 jit_solution(9513128308470783362)
XLA Ops:
  6.5 0.7 fusion.21
  7.3 0.7 fusion.26
  18.1 1.8 broadcast_select_fusion.4
  20.0 0.7 all-gather.11.cloned.1.call-update
  20.8 0.7 all-gather.15.cloned.1.call-update
  22.1 0.9 copy.22
  23.0 0.9 copy.24
  24.8 4.5 collective-permute-start
  29.3 1.9 collective-permute-start.14
  31.2 3.5 collective-permute-start.7
  36.4 1.4 fusion.25
  43.9 2.8 collective-permute-start.1
  47.6 3.5 collective-permute-start.8
  51.1 3.1 collective-permute-start.15
  54.2 3.1 collective-permute-done.1
  57.4 1.9 collective-permute-start.2
  59.3 1.5 collective-permute-done.8
  60.9 1.9 collective-permute-start.9
  62.8 1.0 collective-permute-done.15
  63.8 3.0 collective-permute-start.16
  66.9 3.5 collective-permute-start.3
  70.5 4.7 collective-permute-start.10
  75.3 3.5 collective-permute-start.17
  78.8 4.9 collective-permute-start.4
  83.8 6.3 collective-permute-start.11
  90.1 3.9 collective-permute-start.18
  94.0 5.6 collective-permute-start.5
  99.6 4.7 collective-permute-start.12
  104.3 7.0 collective-permute-start.19
  111.4 7.6 %collective-permute-start.6 = (bf16[1,256,2,128]{3,1,0,2:T(8,128)(2,1)S(1)}, bf16[1,256,2,128]{3,1,0,2:T(8,128)(2,1)S(1)}, u32[]{:S(2)}, u32[]{:S(2)}) collective-permute-start(bf16[1,256,2,128]{3,1,0,2:T(8,128)(2,1)S(1)} %broadcast_select_fusion.24), channel_id=1, source_target_pairs={{0,256},{4,260},{8,264},{12,268},{16,272},{20,276},{24,280},{28,28... | collective-permute-start | bytes 393224 | tf_op jit(solution)/shard_map/ppermute | solution.py:12
  119.0 7.4 %collective-permute-start.13 = (bf16[1,256,2,128]{3,1,0,2:T(8,128)(2,1)S(1)}, bf16[1,256,2,128]{3,1,0,2:T(8,128)(2,1)S(1)}, u32[]{:S(2)}, u32[]{:S(2)}) collective-permute-start(bf16[1,256,2,128]{3,1,0,2:T(8,128)(2,1)S(1)} %broadcast_select_fusion.17), channel_id=1, source_target_pairs={{0,256},{4,260},{8,264},{12,268},{16,272},{20,276},{24,280},{28,28... | collective-permute-start | bytes 393224 | tf_op jit(solution)/shard_map/ppermute | solution.py:12
  126.5 11.7 %collective-permute-start.20 = (bf16[1,256,2,128]{3,1,0,2:T(8,128)(2,1)S(1)}, bf16[1,256,2,128]{3,1,0,2:T(8,128)(2,1)S(1)}, u32[]{:S(2)}, u32[]{:S(2)}) collective-permute-start(bf16[1,256,2,128]{3,1,0,2:T(8,128)(2,1)S(1)} %broadcast_select_fusion.10), channel_id=1, source_target_pairs={{0,256},{4,260},{8,264},{12,268},{16,272},{20,276},{24,280},{28,28... | collective-permute-start | bytes 393224 | tf_op jit(solution)/shard_map/ppermute | solution.py:12
  138.2 1.4 collective-permute-done.6
  139.6 12.6 %collective-permute-done.13 = bf16[1,256,2,128]{3,1,0,2:T(8,128)(2,1)S(1)} collective-permute-done((bf16[1,256,2,128]{3,1,0,2:T(8,128)(2,1)S(1)}, bf16[1,256,2,128]{3,1,0,2:T(8,128)(2,1)S(1)}, u32[]{:S(2)}, u32[]{:S(2)}) %collective-permute-start.13) | collective-permute-done | bytes 131104 | tf_op jit(solution)/shard_map/ppermute | solution.py:12
  152.3 11.8 %collective-permute-done.20 = bf16[1,256,2,128]{3,1,0,2:T(8,128)(2,1)S(1)} collective-permute-done((bf16[1,256,2,128]{3,1,0,2:T(8,128)(2,1)S(1)}, bf16[1,256,2,128]{3,1,0,2:T(8,128)(2,1)S(1)}, u32[]{:S(2)}, u32[]{:S(2)}) %collective-permute-start.20) | collective-permute-done | bytes 131104 | tf_op jit(solution)/shard_map/ppermute | solution.py:12
  164.1 39.2 %all-gather.9.cloned.1.call-done = bf16[16384,2,128]{2,1,0:T(2,128)(2,1)} async-done(((bf16[128,2,128]{2,1,0:T(2,128)(2,1)}), bf16[16384,2,128]{2,1,0:T(2,128)(2,1)}) %all-gather.9.cloned.1.call-update) | async-done | bytes 8388624 | tf_op jit(solution)/shard_map/all_gather | solution.py:17
  203.3 8.7 %reduce_sum.57 = bf16[128,2,128]{2,1,0:T(2,128)(2,1)S(1)} reduce(bf16[128,128,2,128]{3,2,1,0:T(2,128)(2,1)} %bitcast.124, bf16[]{:T(256)} %constant.495.clone.1), dimensions={0}, to_apply=%region_0.1 | reduce | flops 4161536 | bytes 8454146 | tf_op jit(solution)/shard_map/reduce_sum | solution.py:17
  212.1 141.1 %all-gather.11.cloned.1.call-done = bf16[16384,2,128]{2,1,0:T(2,128)(2,1)} async-done(((bf16[128,2,128]{2,1,0:T(2,128)(2,1)}), bf16[16384,2,128]{2,1,0:T(2,128)(2,1)}) %all-gather.11.cloned.1.call-update) | async-done | bytes 8388624 | tf_op jit(solution)/shard_map/all_gather | solution.py:17
  353.2 8.7 %reduce_sum.58 = bf16[128,2,128]{2,1,0:T(2,128)(2,1)S(1)} reduce(bf16[128,128,2,128]{3,2,1,0:T(2,128)(2,1)} %bitcast.125, bf16[]{:T(256)} %constant.495.clone.1), dimensions={0}, to_apply=%region_1.2 | reduce | flops 4161536 | bytes 8454146 | tf_op jit(solution)/shard_map/reduce_sum | solution.py:17
  362.0 136.5 %all-gather.15.cloned.1.call-done = bf16[16384,2,128]{2,1,0:T(2,128)(2,1)} async-done(((bf16[128,2,128]{2,1,0:T(2,128)(2,1)}), bf16[16384,2,128]{2,1,0:T(2,128)(2,1)}) %all-gather.15.cloned.1.call-update) | async-done | bytes 8388624 | tf_op jit(solution)/shard_map/all_gather | solution.py:17
  498.4 8.7 %reduce_sum.60 = bf16[128,2,128]{2,1,0:T(2,128)(2,1)S(1)} reduce(bf16[128,128,2,128]{3,2,1,0:T(2,128)(2,1)} %bitcast.126, bf16[]{:T(256)} %constant.495.clone.1), dimensions={0}, to_apply=%region_3.4 | reduce | flops 4161536 | bytes 8454146 | tf_op jit(solution)/shard_map/reduce_sum | solution.py:17
  507.2 136.3 %all-gather.13.cloned.1.call-done = bf16[16384,2,128]{2,1,0:T(2,128)(2,1)} async-done(((bf16[128,2,128]{2,1,0:T(2,128)(2,1)}), bf16[16384,2,128]{2,1,0:T(2,128)(2,1)}) %all-gather.13.cloned.1.call-update) | async-done | bytes 8388624 | tf_op jit(solution)/shard_map/all_gather | solution.py:17
  643.5 8.7 %reduce_sum.59 = bf16[128,2,128]{2,1,0:T(2,128)(2,1)S(1)} reduce(bf16[128,128,2,128]{3,2,1,0:T(2,128)(2,1)} %bitcast.127, bf16[]{:T(256)} %constant.495.clone.1), dimensions={0}, to_apply=%region_2.3 | reduce | flops 4161536 | bytes 8454146 | tf_op jit(solution)/shard_map/reduce_sum | solution.py:17
  652.9 6.9 fusion.28
  659.8 5.7 fusion.8
  665.5 2.6 fusion.33
  668.2 32.2 %reduce-scatter.2.cloned.1.call-done = f32[256,512]{1,0:T(8,128)} async-done(((f32[256,2048]{1,0:T(8,128)}), f32[256,512]{1,0:T(8,128)}) %reduce-scatter.2.cloned.1.call-update) | async-done | bytes 524304 | tf_op jit(solution)/shard_map/reduce_scatter | solution.py:89
  700.4 1.8 convert_element_type.28
  (64 shorter events, 4.7 us)
Async XLA Ops:
  6.5 646.3 %copy-start = (bf16[256,1024]{1,0:T(8,128)(2,1)S(1)}, bf16[256,1024]{1,0:T(8,128)(2,1)}, u32[]{:S(2)}) copy-start(bf16[256,1024]{1,0:T(8,128)(2,1)} %param.7) | copy-start | bytes 1572868
  6.5 196.8 %all-gather.9.cloned.1.call-start = ((), (), s32[]{:S(2)}) async-start(), calls=%async_computation.2 | async-start | bytes 8454144 | tf_op jit(solution)/shard_map/all_gather | solution.py:17
  20.0 333.2 %all-gather.11.cloned.1.call-start = ((), (), s32[]{:S(2)}) async-start(), calls=%async_computation.3 | async-start | bytes 8454144 | tf_op jit(solution)/shard_map/all_gather | solution.py:17
  20.8 477.7 %all-gather.15.cloned.1.call-start = ((), (), s32[]{:S(2)}) async-start(), calls=%async_computation.5 | async-start | bytes 8454144 | tf_op jit(solution)/shard_map/all_gather | solution.py:17
  21.5 622.0 %all-gather.13.cloned.1.call-start = ((), (), s32[]{:S(2)}) async-start(), calls=%async_computation.4 | async-start | bytes 8454144 | tf_op jit(solution)/shard_map/all_gather | solution.py:17
  22.1 678.3 %reduce-scatter.2.cloned.1.call-start = ((), (), s32[]{:S(2)}) async-start(), calls=%async_computation.1 | async-start | bytes 2621440 | tf_op jit(solution)/shard_map/reduce_scatter | solution.py:89
  24.8 19.0 %collective-permute-start = (bf16[1,256,2,128]{3,1,0,2:T(8,128)(2,1)S(1)}, bf16[1,256,2,128]{3,1,0,2:T(8,128)(2,1)S(1)}, u32[]{:S(2)}, u32[]{:S(2)}) collective-permute-start(bf16[1,256,2,128]{3,1,0,2:T(8,128)(2,1)S(1)} %get-tuple-element.8), channel_id=1, source_target_pairs={{0,4},{4,8},{8,12},{12,16},{16,20},{20,24},{24,28},{28,32},{32,36}... | collective-permute-start | bytes 393224 | tf_op jit(solution)/shard_map/ppermute | solution.py:12
  29.3 14.5 %collective-permute-start.14 = (bf16[1,256,2,128]{3,1,0,2:T(8,128)(2,1)S(1)}, bf16[1,256,2,128]{3,1,0,2:T(8,128)(2,1)S(1)}, u32[]{:S(2)}, u32[]{:S(2)}) collective-permute-start(bf16[1,256,2,128]{3,1,0,2:T(8,128)(2,1)S(1)} %get-tuple-element.9), channel_id=1, source_target_pairs={{0,4},{4,8},{8,12},{12,16},{16,20},{20,24},{24,28},{28,32},{32,36}... | collective-permute-start | bytes 393224 | tf_op jit(solution)/shard_map/ppermute | solution.py:12
  31.2 12.6 %collective-permute-start.7 = (bf16[1,256,2,128]{3,1,0,2:T(8,128)(2,1)S(1)}, bf16[1,256,2,128]{3,1,0,2:T(8,128)(2,1)S(1)}, u32[]{:S(2)}, u32[]{:S(2)}) collective-permute-start(bf16[1,256,2,128]{3,1,0,2:T(8,128)(2,1)S(1)} %get-tuple-element.10), channel_id=1, source_target_pairs={{0,4},{4,8},{8,12},{12,16},{16,20},{20,24},{24,28},{28,32},{32,36}... | collective-permute-start | bytes 393224 | tf_op jit(solution)/shard_map/ppermute | solution.py:12
  43.9 13.5 %collective-permute-start.1 = (bf16[1,256,2,128]{3,1,0,2:T(8,128)(2,1)S(1)}, bf16[1,256,2,128]{3,1,0,2:T(8,128)(2,1)S(1)}, u32[]{:S(2)}, u32[]{:S(2)}) collective-permute-start(bf16[1,256,2,128]{3,1,0,2:T(8,128)(2,1)S(1)} %get-tuple-element.5), channel_id=1, source_target_pairs={{0,8},{4,12},{8,16},{12,20},{16,24},{20,28},{24,32},{28,36},{32,40... | collective-permute-start | bytes 393224 | tf_op jit(solution)/shard_map/ppermute | solution.py:12
  47.6 13.2 %collective-permute-start.8 = (bf16[1,256,2,128]{3,1,0,2:T(8,128)(2,1)S(1)}, bf16[1,256,2,128]{3,1,0,2:T(8,128)(2,1)S(1)}, u32[]{:S(2)}, u32[]{:S(2)}) collective-permute-start(bf16[1,256,2,128]{3,1,0,2:T(8,128)(2,1)S(1)} %get-tuple-element.6), channel_id=1, source_target_pairs={{0,8},{4,12},{8,16},{12,20},{16,24},{20,28},{24,32},{28,36},{32,40... | collective-permute-start | bytes 393224 | tf_op jit(solution)/shard_map/ppermute | solution.py:12
  51.1 12.7 %collective-permute-start.15 = (bf16[1,256,2,128]{3,1,0,2:T(8,128)(2,1)S(1)}, bf16[1,256,2,128]{3,1,0,2:T(8,128)(2,1)S(1)}, u32[]{:S(2)}, u32[]{:S(2)}) collective-permute-start(bf16[1,256,2,128]{3,1,0,2:T(8,128)(2,1)S(1)} %get-tuple-element.7), channel_id=1, source_target_pairs={{0,8},{4,12},{8,16},{12,20},{16,24},{20,28},{24,32},{28,36},{32,40... | collective-permute-start | bytes 393224 | tf_op jit(solution)/shard_map/ppermute | solution.py:12
  57.4 9.5 %collective-permute-start.2 = (bf16[1,256,2,128]{3,1,0,2:T(8,128)(2,1)S(1)}, bf16[1,256,2,128]{3,1,0,2:T(8,128)(2,1)S(1)}, u32[]{:S(2)}, u32[]{:S(2)}) collective-permute-start(bf16[1,256,2,128]{3,1,0,2:T(8,128)(2,1)S(1)} %broadcast_select_fusion.20), channel_id=1, source_target_pairs={{0,16},{4,20},{8,24},{12,28},{16,32},{20,36},{24,40},{28,44},{32,4... | collective-permute-start | bytes 393224 | tf_op jit(solution)/shard_map/ppermute | solution.py:12
  60.9 9.6 %collective-permute-start.9 = (bf16[1,256,2,128]{3,1,0,2:T(8,128)(2,1)S(1)}, bf16[1,256,2,128]{3,1,0,2:T(8,128)(2,1)S(1)}, u32[]{:S(2)}, u32[]{:S(2)}) collective-permute-start(bf16[1,256,2,128]{3,1,0,2:T(8,128)(2,1)S(1)} %broadcast_select_fusion.13), channel_id=1, source_target_pairs={{0,16},{4,20},{8,24},{12,28},{16,32},{20,36},{24,40},{28,44},{32,4... | collective-permute-start | bytes 393224 | tf_op jit(solution)/shard_map/ppermute | solution.py:12
  63.8 11.4 %collective-permute-start.16 = (bf16[1,256,2,128]{3,1,0,2:T(8,128)(2,1)S(1)}, bf16[1,256,2,128]{3,1,0,2:T(8,128)(2,1)S(1)}, u32[]{:S(2)}, u32[]{:S(2)}) collective-permute-start(bf16[1,256,2,128]{3,1,0,2:T(8,128)(2,1)S(1)} %broadcast_select_fusion.6), channel_id=1, source_target_pairs={{0,16},{4,20},{8,24},{12,28},{16,32},{20,36},{24,40},{28,44},{32,4... | collective-permute-start | bytes 393224 | tf_op jit(solution)/shard_map/ppermute | solution.py:12
  66.9 11.9 %collective-permute-start.3 = (bf16[1,256,2,128]{3,1,0,2:T(8,128)(2,1)S(1)}, bf16[1,256,2,128]{3,1,0,2:T(8,128)(2,1)S(1)}, u32[]{:S(2)}, u32[]{:S(2)}) collective-permute-start(bf16[1,256,2,128]{3,1,0,2:T(8,128)(2,1)S(1)} %broadcast_select_fusion.21), channel_id=1, source_target_pairs={{0,32},{4,36},{8,40},{12,44},{16,48},{20,52},{24,56},{28,60},{32,6... | collective-permute-start | bytes 393224 | tf_op jit(solution)/shard_map/ppermute | solution.py:12
  70.5 13.3 %collective-permute-start.10 = (bf16[1,256,2,128]{3,1,0,2:T(8,128)(2,1)S(1)}, bf16[1,256,2,128]{3,1,0,2:T(8,128)(2,1)S(1)}, u32[]{:S(2)}, u32[]{:S(2)}) collective-permute-start(bf16[1,256,2,128]{3,1,0,2:T(8,128)(2,1)S(1)} %broadcast_select_fusion.14), channel_id=1, source_target_pairs={{0,32},{4,36},{8,40},{12,44},{16,48},{20,52},{24,56},{28,60},{32,6... | collective-permute-start | bytes 393224 | tf_op jit(solution)/shard_map/ppermute | solution.py:12
  75.3 14.8 %collective-permute-start.17 = (bf16[1,256,2,128]{3,1,0,2:T(8,128)(2,1)S(1)}, bf16[1,256,2,128]{3,1,0,2:T(8,128)(2,1)S(1)}, u32[]{:S(2)}, u32[]{:S(2)}) collective-permute-start(bf16[1,256,2,128]{3,1,0,2:T(8,128)(2,1)S(1)} %broadcast_select_fusion.7), channel_id=1, source_target_pairs={{0,32},{4,36},{8,40},{12,44},{16,48},{20,52},{24,56},{28,60},{32,6... | collective-permute-start | bytes 393224 | tf_op jit(solution)/shard_map/ppermute | solution.py:12
  78.8 15.1 %collective-permute-start.4 = (bf16[1,256,2,128]{3,1,0,2:T(8,128)(2,1)S(1)}, bf16[1,256,2,128]{3,1,0,2:T(8,128)(2,1)S(1)}, u32[]{:S(2)}, u32[]{:S(2)}) collective-permute-start(bf16[1,256,2,128]{3,1,0,2:T(8,128)(2,1)S(1)} %broadcast_select_fusion.22), channel_id=1, source_target_pairs={{0,64},{4,68},{8,72},{12,76},{16,80},{20,84},{24,88},{28,92},{32,9... | collective-permute-start | bytes 393224 | tf_op jit(solution)/shard_map/ppermute | solution.py:12
  83.8 15.8 %collective-permute-start.11 = (bf16[1,256,2,128]{3,1,0,2:T(8,128)(2,1)S(1)}, bf16[1,256,2,128]{3,1,0,2:T(8,128)(2,1)S(1)}, u32[]{:S(2)}, u32[]{:S(2)}) collective-permute-start(bf16[1,256,2,128]{3,1,0,2:T(8,128)(2,1)S(1)} %broadcast_select_fusion.15), channel_id=1, source_target_pairs={{0,64},{4,68},{8,72},{12,76},{16,80},{20,84},{24,88},{28,92},{32,9... | collective-permute-start | bytes 393224 | tf_op jit(solution)/shard_map/ppermute | solution.py:12
  90.1 14.2 %collective-permute-start.18 = (bf16[1,256,2,128]{3,1,0,2:T(8,128)(2,1)S(1)}, bf16[1,256,2,128]{3,1,0,2:T(8,128)(2,1)S(1)}, u32[]{:S(2)}, u32[]{:S(2)}) collective-permute-start(bf16[1,256,2,128]{3,1,0,2:T(8,128)(2,1)S(1)} %broadcast_select_fusion.8), channel_id=1, source_target_pairs={{0,64},{4,68},{8,72},{12,76},{16,80},{20,84},{24,88},{28,92},{32,9... | collective-permute-start | bytes 393224 | tf_op jit(solution)/shard_map/ppermute | solution.py:12
  94.0 17.4 %collective-permute-start.5 = (bf16[1,256,2,128]{3,1,0,2:T(8,128)(2,1)S(1)}, bf16[1,256,2,128]{3,1,0,2:T(8,128)(2,1)S(1)}, u32[]{:S(2)}, u32[]{:S(2)}) collective-permute-start(bf16[1,256,2,128]{3,1,0,2:T(8,128)(2,1)S(1)} %broadcast_select_fusion.23), channel_id=1, source_target_pairs={{0,128},{4,132},{8,136},{12,140},{16,144},{20,148},{24,152},{28,15... | collective-permute-start | bytes 393224 | tf_op jit(solution)/shard_map/ppermute | solution.py:12
  99.6 19.4 %collective-permute-start.12 = (bf16[1,256,2,128]{3,1,0,2:T(8,128)(2,1)S(1)}, bf16[1,256,2,128]{3,1,0,2:T(8,128)(2,1)S(1)}, u32[]{:S(2)}, u32[]{:S(2)}) collective-permute-start(bf16[1,256,2,128]{3,1,0,2:T(8,128)(2,1)S(1)} %broadcast_select_fusion.16), channel_id=1, source_target_pairs={{0,128},{4,132},{8,136},{12,140},{16,144},{20,148},{24,152},{28,15... | collective-permute-start | bytes 393224 | tf_op jit(solution)/shard_map/ppermute | solution.py:12
  104.3 22.1 %collective-permute-start.19 = (bf16[1,256,2,128]{3,1,0,2:T(8,128)(2,1)S(1)}, bf16[1,256,2,128]{3,1,0,2:T(8,128)(2,1)S(1)}, u32[]{:S(2)}, u32[]{:S(2)}) collective-permute-start(bf16[1,256,2,128]{3,1,0,2:T(8,128)(2,1)S(1)} %broadcast_select_fusion.9), channel_id=1, source_target_pairs={{0,128},{4,132},{8,136},{12,140},{16,144},{20,148},{24,152},{28,15... | collective-permute-start | bytes 393224 | tf_op jit(solution)/shard_map/ppermute | solution.py:12
  111.4 28.2 %collective-permute-start.6 = (bf16[1,256,2,128]{3,1,0,2:T(8,128)(2,1)S(1)}, bf16[1,256,2,128]{3,1,0,2:T(8,128)(2,1)S(1)}, u32[]{:S(2)}, u32[]{:S(2)}) collective-permute-start(bf16[1,256,2,128]{3,1,0,2:T(8,128)(2,1)S(1)} %broadcast_select_fusion.24), channel_id=1, source_target_pairs={{0,256},{4,260},{8,264},{12,268},{16,272},{20,276},{24,280},{28,28... | collective-permute-start | bytes 393224 | tf_op jit(solution)/shard_map/ppermute | solution.py:12
  119.0 33.2 %collective-permute-start.13 = (bf16[1,256,2,128]{3,1,0,2:T(8,128)(2,1)S(1)}, bf16[1,256,2,128]{3,1,0,2:T(8,128)(2,1)S(1)}, u32[]{:S(2)}, u32[]{:S(2)}) collective-permute-start(bf16[1,256,2,128]{3,1,0,2:T(8,128)(2,1)S(1)} %broadcast_select_fusion.17), channel_id=1, source_target_pairs={{0,256},{4,260},{8,264},{12,268},{16,272},{20,276},{24,280},{28,28... | collective-permute-start | bytes 393224 | tf_op jit(solution)/shard_map/ppermute | solution.py:12
  126.5 37.6 %collective-permute-start.20 = (bf16[1,256,2,128]{3,1,0,2:T(8,128)(2,1)S(1)}, bf16[1,256,2,128]{3,1,0,2:T(8,128)(2,1)S(1)}, u32[]{:S(2)}, u32[]{:S(2)}) collective-permute-start(bf16[1,256,2,128]{3,1,0,2:T(8,128)(2,1)S(1)} %broadcast_select_fusion.10), channel_id=1, source_target_pairs={{0,256},{4,260},{8,264},{12,268},{16,272},{20,276},{24,280},{28,28... | collective-permute-start | bytes 393224 | tf_op jit(solution)/shard_map/ppermute | solution.py:12
  659.8 5.8 copy-start.1
Sparse Core Ops, SparseCore 0:
  20.1 183.1 all-gather.8
  206.5 146.6 all-gather.10
  356.4 142.0 all-gather.14
  501.4 142.0 all-gather.12
  668.3 32.0 reduce-scatter.1
